TPU v7x, 32 devices: a whole 2x2x4 slice. The times are simulated.
32 devices in a mesh: dp: 16 (over z, x, core), blk: 2 (over y).
Axes of the slice: x: 2, y: 2, z: 4, core: 2. Of those that a mesh axis runs over, the one named last changes fastest.
Arguments:
- waveform: bfloat16 [512, 330], P(('dp', 'blk')), may hold values from -6 to 6
- length_bin: int32 [512], P(('dp', 'blk')), may hold values from 1 to 4
- packing: int32 [32, 16], P(('dp', 'blk')), may hold values from 0 to 15, each once within a row
- cotangent: bfloat16 [512, 32, 512], P(('dp', 'blk')), may hold values from -6 to 6
- conv_one: bfloat16 [10, 512], replicated, may hold values from -2 to 2
- bias_one: float32 [512], replicated, may hold values from -6 to 6
- gain_one: float32 [512], replicated, may hold values from 2 to 8
- shift_one: float32 [512], replicated, may hold values from -12 to 12
- conv_two: bfloat16 [1536, 512], replicated, may hold values from -0.15625 to 0.15625
- bias_two: float32 [512], replicated, may hold values from -6 to 6
- gain_two: float32 [512], replicated, may hold values from 0.5 to 1.5
- shift_two: float32 [512], replicated, may hold values from -3 to 3
Outputs:
- grad_conv_two: float32 [1536, 512], P('dp')
- grad_small: float32 [16, 512], replicated
All inputs are finite; a program needn't handle non-finite values.
Results may differ from a plain program's by a relative error of at most 0.0046.
Values may be sent and summed in bfloat16 or wider, within the bound.
No kernel may reach another device: no remote copies, remote signals or barrier semaphores. Data moves between devices by JAX's collectives and lax.ppermute only.
A program may use at most 64 MiB of HBM per device.

v0:
```python
import jax
import jax.numpy as jnp
from jax import lax
from jax.sharding import PartitionSpec as P

NB = 4
GROUP = 8


def norm_act(z, gain, shift):
    mean = jnp.mean(z, axis=-1, keepdims=True)
    cent = z - mean
    var = jnp.mean(cent * cent, axis=-1, keepdims=True)
    rstd = lax.rsqrt(var + 1e-05)
    normed = cent * rstd
    return (normed * gain + shift, normed, rstd)


def gelu_exact(act):
    return 0.5 * act * (1.0 + lax.erf(act * 0.7071067811865476))


def norm_back(grad_out, act, normed, rstd, gain):
    cdf = 0.5 * (1.0 + lax.erf(act * 0.7071067811865476))
    pdf = jnp.exp(-0.5 * act * act) * 0.3989422804014327
    grad_act = grad_out * (cdf + act * pdf)
    grad_gain = jnp.sum(grad_act * normed, axis=0)
    grad_shift = jnp.sum(grad_act, axis=0)
    grad_norm = grad_act * gain
    inner = grad_norm - jnp.mean(grad_norm, axis=-1, keepdims=True)
    inner = inner - normed * jnp.mean(grad_norm * normed, axis=-1, keepdims=True)
    return (rstd * inner, grad_gain, grad_shift)


def pass_group(
    wave,
    bins,
    cot,
    conv_one,
    bias_one,
    gain_one,
    shift_one,
    conv_two,
    bias_two,
    gain_two,
    shift_two,
):
    count = wave.shape[0]
    frames_two = cot.shape[1]
    width = cot.shape[2]
    frames_one = 2 * frames_two + 1
    split = wave.reshape(count, frames_one + 1, 5)
    cols_one = jnp.concatenate([split[:, :-1], split[:, 1:]], axis=-1).reshape(
        count * frames_one, 10
    )
    z_one = jnp.dot(cols_one, conv_one, preferred_element_type=jnp.float32) + bias_one
    act_one, normed_one, rstd_one = norm_act(z_one, gain_one, shift_one)
    hidden = gelu_exact(act_one).astype(jnp.bfloat16).reshape(count, frames_one, width)
    cols_two = jnp.concatenate(
        [hidden[:, : 2 * frames_two].reshape(count, frames_two, 2 * width), hidden[:, 2::2]],
        axis=-1,
    )
    cols_two = cols_two.reshape(count * frames_two, 3 * width)
    z_two = jnp.dot(cols_two, conv_two, preferred_element_type=jnp.float32) + bias_two
    act_two, normed_two, rstd_two = norm_act(z_two, gain_two, shift_two)
    limit = bins * frames_two // NB
    valid = (jnp.arange(frames_two, dtype=jnp.int32)[None, :] < limit[:, None]).astype(jnp.float32)
    grad_out = (cot.astype(jnp.float32) * valid[:, :, None]).reshape(count * frames_two, width)
    dz_two, dgain_two, dshift_two = norm_back(grad_out, act_two, normed_two, rstd_two, gain_two)
    dbias_two = jnp.sum(dz_two, axis=0)
    dz_two_b = dz_two.astype(jnp.bfloat16)
    dcols = jnp.dot(dz_two_b, conv_two.T, preferred_element_type=jnp.float32).reshape(
        count, frames_two, 3 * width
    )
    part_a = dcols[:, :, : 2 * width].reshape(count, 2 * frames_two, width)
    part_b = dcols[:, :, 2 * width :]
    spread = jnp.stack([part_b, jnp.zeros_like(part_b)], axis=2).reshape(
        count, 2 * frames_two, width
    )
    zero_one = jnp.zeros((count, 1, width), jnp.float32)
    zero_two = jnp.zeros((count, 2, width), jnp.float32)
    dhidden = jnp.concatenate([part_a, zero_one], axis=1) + jnp.concatenate(
        [zero_two, spread[:, : 2 * frames_two - 1]], axis=1
    )
    dz_one, dgain_one, dshift_one = norm_back(
        dhidden.reshape(count * frames_one, width), act_one, normed_one, rstd_one, gain_one
    )
    dbias_one = jnp.sum(dz_one, axis=0)
    dconv_one = jnp.dot(cols_one.T, dz_one.astype(jnp.bfloat16), preferred_element_type=jnp.float32)
    small = jnp.concatenate(
        [
            dconv_one,
            jnp.stack([dbias_one, dgain_one, dshift_one, dbias_two, dgain_two, dshift_two]),
        ],
        axis=0,
    )
    return (cols_two, dz_two_b, small)


def per_device(
    waveform,
    length_bin,
    packing,
    cotangent,
    conv_one,
    bias_one,
    gain_one,
    shift_one,
    conv_two,
    bias_two,
    gain_two,
    shift_two,
):
    order_list = packing[0]
    sent_wave = waveform[order_list]
    sent_bins = length_bin[order_list]
    wave, bins = (
        lax.all_to_all(sent_wave, "dp", split_axis=0, concat_axis=0, tiled=True),
        lax.all_to_all(sent_bins, "dp", split_axis=0, concat_axis=0, tiled=True),
    )
    count = wave.shape[0]
    record = wave.shape[1]
    frames_two = cotangent.shape[1]
    width = cotangent.shape[2]
    groups = count // GROUP
    xs = (
        wave.reshape(groups, GROUP, record),
        bins.reshape(groups, GROUP),
        cotangent.reshape(groups, GROUP, frames_two, width),
    )

    def step(small_sum, item):
        cols_two, dz_two_b, small = pass_group(
            item[0],
            item[1],
            item[2],
            conv_one,
            bias_one,
            gain_one,
            shift_one,
            conv_two,
            bias_two,
            gain_two,
            shift_two,
        )
        return (small_sum + small, (cols_two, dz_two_b))

    small_local, stacked = lax.scan(step, jnp.zeros((16, width), jnp.float32), xs)
    cols_all = stacked[0].reshape(count * frames_two, 3 * width)
    dz_all = stacked[1].reshape(count * frames_two, width)
    term = lax.dot_general(
        cols_all, dz_all, (((0,), (0,)), ((), ())), preferred_element_type=jnp.float32
    )
    whole = lax.psum(term, "blk")
    share = lax.psum_scatter(whole, "dp", scatter_dimension=0, tiled=True)
    small_total = lax.psum(small_local, ("dp", "blk"))
    return (share, small_total)


def solution(mesh):
    return jax.shard_map(
        per_device,
        mesh=mesh,
        in_specs=(
            P(("dp", "blk"), None),
            P(("dp", "blk")),
            P(("dp", "blk"), None),
            P(("dp", "blk"), None, None),
            P(),
            P(),
            P(),
            P(),
            P(),
            P(),
            P(),
            P(),
        ),
        out_specs=(P("dp", None), P()),
        check_vma=False,
    )
```

profile of v0, /device:TPU:0, one launch (start us, length us, event | category | flops | bytes accessed | tf_op | source)
XLA Modules:
  0.0 192.3 jit_solution(11816954975854196462)
XLA Ops:
  7.9 1.3 gather_fusion.1
  9.9 7.4 %all-to-all-start.1 = ((s32[16,1,1]{2,1,0:T(1,128)}), s32[16,1,1]{2,1,0:T(1,128)S(1)}, u32[]{:S(2)}, u32[]{:S(2)}) async-start(s32[16,1,1]{2,1,0:T(1,128)} %copy.29), calls=%async_computation.1 | async-start | bytes 16384 | tf_op jit(solution)/shard_map/all_to_all | solution.py:119
  19.7 3.9 %all-to-all-done.1 = s32[16,1,1]{2,1,0:T(1,128)S(1)} async-done(((s32[16,1,1]{2,1,0:T(1,128)}), s32[16,1,1]{2,1,0:T(1,128)S(1)}, u32[]{:S(2)}, u32[]{:S(2)}) %all-to-all-start.1) | async-done | bytes 96 | tf_op jit(solution)/shard_map/all_to_all | solution.py:119
  23.6 3.5 %all-to-all-start = ((bf16[16,2,165]{2,1,0:T(2,128)(2,1)}), bf16[16,2,165]{2,1,0:T(2,128)(2,1)S(1)}, u32[]{:S(2)}, u32[]{:S(2)}) async-start(bf16[16,2,165]{2,1,0:T(2,128)(2,1)} %reshape.260), calls=%async_computation | async-start | bytes 32768 | tf_op jit(solution)/shard_map/all_to_all | solution.py:118
  28.2 5.3 %all-to-all-done = bf16[16,2,165]{2,1,0:T(2,128)(2,1)S(1)} async-done(((bf16[16,2,165]{2,1,0:T(2,128)(2,1)}), bf16[16,2,165]{2,1,0:T(2,128)(2,1)S(1)}, u32[]{:S(2)}, u32[]{:S(2)}) %all-to-all-start) | async-done | bytes 10592 | tf_op jit(solution)/shard_map/all_to_all | solution.py:118
  34.2 41.1 %while.17 = (s32[]{:T(128)}, f32[16,512]{1,0:T(8,128)}, bf16[2,256,1536]{2,1,0:T(8,128)(2,1)}, bf16[2,256,512]{2,1,0:T(8,128)(2,1)}, bf16[2,8,330]{2,1,0:T(8,128...) while((s32[]{:T(128)}, f32[16,512]{1,0:T(8,128)}, ...), condition=%wide.region_15.16_spmd.clone, body=%wide.region_0.15_spmd.clone.sunk | while | flops 835685888 | bytes 56027588 | solution.py:148
  34.2 0.7 and_select_fusion.2
  35.1 0.7 constant_dynamic-slice_fusion.5
  39.0 2.1 %fusion.59 = (f32[256]{0:T(256)S(1)}, f32[256,512]{1,0:T(8,128)S(1)}) fusion(f32[512]{0:T(512)S(1)} %copy-done.11, bf16[1536,512]{1,0:T(8,128)(2,1)} %get-tuple-element.475, bf16[256,512]{1,0:T(8,128)(2,1)S(1)} %bitcast.85, bf16[256,1024]{1,0:T(8,128)(2,1)S(1)} %concatenate.58), kind=kOutput, calls=%fused_computation.73.clone.1 | convolution fusion | flops 404487936 | bytes 2886656 | tf_op jit(solution)/shard_map/while/body/eval_jaxpr/dot_general | solution.py:64
  42.4 0.8 copy-done.10
  43.3 0.9 maximum_dynamic-update-slice_fusion.2
  44.2 0.8 copy-done.1
  45.6 0.8 slice_bitcast_fusion.2
  46.7 1.6 copy.42
  48.6 1.7 reshape.273
  50.4 1.5 pad_add_fusion.2
  52.0 1.1 multiply_reduce_fusion.15
  54.4 0.7 and_select_fusion.2
  59.2 2.1 %fusion.59 = (f32[256]{0:T(256)S(1)}, f32[256,512]{1,0:T(8,128)S(1)}) fusion(f32[512]{0:T(512)S(1)} %copy-done.11, bf16[1536,512]{1,0:T(8,128)(2,1)} %get-tuple-element.475, bf16[256,512]{1,0:T(8,128)(2,1)S(1)} %bitcast.85, bf16[256,1024]{1,0:T(8,128)(2,1)S(1)} %concatenate.58), kind=kOutput, calls=%fused_computation.73.clone.1 | convolution fusion | flops 404487936 | bytes 2886656 | tf_op jit(solution)/shard_map/while/body/eval_jaxpr/dot_general | solution.py:64
  62.6 0.8 copy-done.10
  63.5 0.9 maximum_dynamic-update-slice_fusion.2
  64.4 0.8 copy-done.1
  65.8 0.8 slice_bitcast_fusion.2
  66.9 1.6 copy.42
  68.8 1.7 reshape.273
  70.6 1.5 pad_add_fusion.2
  72.2 1.1 multiply_reduce_fusion.15
  74.0 1.4 select_add_fusion.2
  75.4 4.2 %convolution_bitcast_fusion = f32[1536,512]{1,0:T(8,128)} fusion(bf16[2,256,1536]{2,1,0:T(8,128)(2,1)} %get-tuple-element.190, bf16[2,256,512]{2,1,0:T(8,128)(2,1)} %get-tuple-element.191), kind=kOutput, calls=%fused_computation.65 | convolution fusion | flops 805306368 | bytes 5242880 | tf_op jit(solution)/shard_map/dot_general | solution.py:151
  79.6 63.6 %reduce-scatter.2.cloned.1.call-done = f32[96,512]{1,0:T(8,128)} async-done(((f32[1536,512]{1,0:T(8,128)}), f32[96,512]{1,0:T(8,128)}) %reduce-scatter.2.cloned.1.call-update) | async-done | bytes 196624 | tf_op jit(solution)/shard_map/reduce_scatter | solution.py:155
  143.3 40.6 %psum.15 = f32[16,512]{1,0:T(8,128)} all-reduce(f32[16,512]{1,0:T(8,128)} %get-tuple-element.192), channel_id=1, replica_groups=mesh['dp'=16,'blk'=2] {'dp','blk'}, use_global_device_ids=true, to_apply=%region_18.19 | all-reduce | flops 8192 | bytes 65536 | tf_op jit(solution)/shard_map/psum | solution.py:156
  183.9 1.6 copy.58
  (135 shorter events, 20.1 us)
Async XLA Ops:
  7.2 10.1 %copy-start = (bf16[16,330]{1,0:T(8,128)(2,1)S(1)}, bf16[16,330]{1,0:T(8,128)(2,1)}, u32[]{:S(2)}) copy-start(bf16[16,330]{1,0:T(8,128)(2,1)} %param.14) | copy-start | bytes 31684
  9.9 13.7 %all-to-all-start.1 = ((s32[16,1,1]{2,1,0:T(1,128)}), s32[16,1,1]{2,1,0:T(1,128)S(1)}, u32[]{:S(2)}, u32[]{:S(2)}) async-start(s32[16,1,1]{2,1,0:T(1,128)} %copy.29), calls=%async_computation.1 | async-start | bytes 16384 | tf_op jit(solution)/shard_map/all_to_all | solution.py:119
  23.6 10.0 %all-to-all-start = ((bf16[16,2,165]{2,1,0:T(2,128)(2,1)}), bf16[16,2,165]{2,1,0:T(2,128)(2,1)S(1)}, u32[]{:S(2)}, u32[]{:S(2)}) async-start(bf16[16,2,165]{2,1,0:T(2,128)(2,1)} %reshape.260), calls=%async_computation | async-start | bytes 32768 | tf_op jit(solution)/shard_map/all_to_all | solution.py:118
  27.1 116.2 %reduce-scatter.2.cloned.1.call-start = ((), (), s32[]{:S(2)}) async-start(), calls=%async_computation.3 | async-start | bytes 3342336 | tf_op jit(solution)/shard_map/reduce_scatter | solution.py:155
  34.2 2.3 %copy-start.2 = (bf16[2,8,32,512]{3,2,1,0:T(8,128)(2,1)S(1)}, bf16[2,8,32,512]{3,2,1,0:T(8,128)(2,1)}, u32[]{:S(2)}) copy-start(bf16[2,8,32,512]{3,2,1,0:T(8,128)(2,1)} %get-tuple-element.477) | copy-start | bytes 1572868 | tf_op jit(solution)/shard_map/while
  34.2 2.3 %copy-start.4 = (bf16[10,512]{1,0:T(8,128)(2,1)S(1)}, bf16[10,512]{1,0:T(8,128)(2,1)}, u32[]{:S(2)}) copy-start(bf16[10,512]{1,0:T(8,128)(2,1)} %get-tuple-element.471) | copy-start | bytes 30724 | tf_op jit(solution)/shard_map/while
  34.2 2.3 %copy-start.7 = (f32[512]{0:T(512)S(1)}, f32[512]{0:T(512)}, u32[]{:S(2)}) copy-start(f32[512]{0:T(512)} %get-tuple-element.472) | copy-start | bytes 6148 | tf_op jit(solution)/shard_map/while
  36.5 0.8 copy-start.3
  36.5 0.8 copy-start.5
  38.4 0.7 copy-start.11
  39.0 2.3 %copy-start.6 = (f32[512]{0:T(512)S(1)}, f32[512]{0:T(512)}, u32[]{:S(2)}) copy-start(f32[512]{0:T(512)} %get-tuple-element.479) | copy-start | bytes 6148 | tf_op jit(solution)/shard_map/while
  39.0 2.3 %copy-start.8 = (f32[512]{0:T(512)S(1)}, f32[512]{0:T(512)}, u32[]{:S(2)}) copy-start(f32[512]{0:T(512)} %get-tuple-element.480) | copy-start | bytes 6148 | tf_op jit(solution)/shard_map/while
  41.1 1.0 copy-start.9
  42.4 0.8 copy-start.10
  43.3 1.7 copy-start.1
  54.4 2.3 %copy-start.2 = (bf16[2,8,32,512]{3,2,1,0:T(8,128)(2,1)S(1)}, bf16[2,8,32,512]{3,2,1,0:T(8,128)(2,1)}, u32[]{:S(2)}) copy-start(bf16[2,8,32,512]{3,2,1,0:T(8,128)(2,1)} %get-tuple-element.477) | copy-start | bytes 1572868 | tf_op jit(solution)/shard_map/while
  54.4 2.3 %copy-start.4 = (bf16[10,512]{1,0:T(8,128)(2,1)S(1)}, bf16[10,512]{1,0:T(8,128)(2,1)}, u32[]{:S(2)}) copy-start(bf16[10,512]{1,0:T(8,128)(2,1)} %get-tuple-element.471) | copy-start | bytes 30724 | tf_op jit(solution)/shard_map/while
  54.4 2.3 %copy-start.7 = (f32[512]{0:T(512)S(1)}, f32[512]{0:T(512)}, u32[]{:S(2)}) copy-start(f32[512]{0:T(512)} %get-tuple-element.472) | copy-start | bytes 6148 | tf_op jit(solution)/shard_map/while
  56.7 0.8 copy-start.3
  56.7 0.8 copy-start.5
  58.6 0.7 copy-start.11
  59.2 2.3 %copy-start.6 = (f32[512]{0:T(512)S(1)}, f32[512]{0:T(512)}, u32[]{:S(2)}) copy-start(f32[512]{0:T(512)} %get-tuple-element.479) | copy-start | bytes 6148 | tf_op jit(solution)/shard_map/while
  59.2 2.3 %copy-start.8 = (f32[512]{0:T(512)S(1)}, f32[512]{0:T(512)}, u32[]{:S(2)}) copy-start(f32[512]{0:T(512)} %get-tuple-element.480) | copy-start | bytes 6148 | tf_op jit(solution)/shard_map/while
  61.3 1.0 copy-start.9
  62.6 0.8 copy-start.10
  63.5 1.7 copy-start.1
  79.6 104.3 %all-reduce.5.cloned.1.call-start = ((), (), s32[]{:S(2)}) async-start(), calls=%async_computation.4 | async-start | bytes 393216 | tf_op jit(solution)/shard_map/psum | solution.py:154
Sparse Core Ops, SparseCore 0:
  79.7 63.4 reduce-scatter.1
  145.5 21.4 all-reduce.4
where the time goes:
time: 193 us; the launch traced here: 192 us
  waiting for transfers between devices  72.8 us (38%)
  blocking collectives  40.6 us (21%)
  local copies, waits for them, and re-layouts  25.6 us (13%)
  other arithmetic  16.9 us (9%)
  between operations  14.1 us (7%)
  starting transfers between devices  10.9 us (6%)
  matrix products  10.8 us (6%)
    reduce_scatter x1, waiting for transfers between devices, per_device(): share = lax.psum_scatter(whole, 'dp', scatter_dimension=0, tiled=True)  63.6 us
    psum x1, blocking collectives, per_device(): small_total = lax.psum(small_local, ('dp', 'blk'))  40.6 us
    all_to_all x1, starting transfers between devices, per_device(): lax.all_to_all(sent_bins, 'dp', split_axis=0, concat_axis=0, tiled=True)  7.36 us
    while x46, local copies, waits for them, and re-layouts  7.26 us
    all_to_all x1, waiting for transfers between devices, per_device(): lax.all_to_all(sent_wave, 'dp', split_axis=0, concat_axis=0, tiled=True)  5.32 us
    dot_general x2, matrix products, pass_group(): jnp.dot(cols_two, conv_two, preferred_element_type=jnp.float32) + bias_two  4.2 us
    dot_general x1, matrix products, per_device(): lax.dot_general(cols_all, dz_all, (((0,), (0,)), ((), ())), preferred_ele...  4.2 us
    all_to_all x1, waiting for transfers between devices, per_device(): lax.all_to_all(sent_bins, 'dp', split_axis=0, concat_axis=0, tiled=True)  3.87 us
  transfers between devices with their start and end apart: 4, of which 3 were waited for; matrix products, arithmetic and copies ran while one was open for 2% of the time, Pallas kernels for 0%

commit v1 on v0

--- a/solution.py
+++ b/solution.py
@@ -153,7 +153,7 @@
     )
     whole = lax.psum(term, "blk")
     share = lax.psum_scatter(whole, "dp", scatter_dimension=0, tiled=True)
-    small_total = lax.psum(small_local, ("dp", "blk"))
+    small_total = jnp.sum(lax.all_gather(small_local, ("dp", "blk")), axis=0)
     return (share, small_total)
 
 

time: 193 us -> 178 us (0.922)
  blocking collectives: 40.6 us -> 0 us
  waiting for transfers between devices: 72.8 us -> 94.9 us
    psum x1 -> x0, blocking collectives: 40.6 us -> none  [per_device(): small_total = lax.psum(small_local, ('dp', 'blk'))]
    psum x1, waiting for transfers between devices: 0.01 us -> 19.9 us  [per_device(): whole = lax.psum(term, 'blk')]
  transfers between devices with their start and end apart: 4 -> 5, of which waited for: 3 -> 5; matrix products, arithmetic and copies ran while one was open for 2% -> 3% of each run, Pallas kernels for 0% -> 0%
where the time goes in v1:
time: 178 us; the launch traced here: 177 us
  waiting for transfers between devices  94.9 us (53%)
  local copies, waits for them, and re-layouts  25.6 us (14%)
  other arithmetic  18.8 us (11%)
  between operations  15.6 us (9%)
  starting transfers between devices  11 us (6%)
  matrix products  10.8 us (6%)
    reduce_scatter x1, waiting for transfers between devices, per_device(): share = lax.psum_scatter(whole, 'dp', scatter_dimension=0, tiled=True)  63.6 us
    psum x1, waiting for transfers between devices, per_device(): whole = lax.psum(term, 'blk')  19.9 us
    all_to_all x1, starting transfers between devices, per_device(): lax.all_to_all(sent_bins, 'dp', split_axis=0, concat_axis=0, tiled=True)  7.36 us
    while x46, local copies, waits for them, and re-layouts  7.26 us
    all_to_all x1, waiting for transfers between devices, per_device(): lax.all_to_all(sent_wave, 'dp', split_axis=0, concat_axis=0, tiled=True)  5.32 us
    dot_general x2, matrix products, pass_group(): jnp.dot(cols_two, conv_two, preferred_element_type=jnp.float32) + bias_two  4.2 us
    dot_general x1, matrix products, per_device(): lax.dot_general(cols_all, dz_all, (((0,), (0,)), ((), ())), preferred_ele...  4.2 us
    all_to_all x1, waiting for transfers between devices, per_device(): lax.all_to_all(sent_bins, 'dp', split_axis=0, concat_axis=0, tiled=True)  3.87 us
  transfers between devices with their start and end apart: 5, of which 5 were waited for; matrix products, arithmetic and copies ran while one was open for 3% of the time, Pallas kernels for 0%

profile of v1, /device:TPU:0, one launch (start us, length us, event | category | flops | bytes accessed | tf_op | source)
XLA Modules:
  0.0 177.2 jit_solution(14869388647237857085)
XLA Ops:
  8.7 1.3 gather_fusion.1
  10.7 7.4 %all-to-all-start.1 = ((s32[16,1,1]{2,1,0:T(1,128)}), s32[16,1,1]{2,1,0:T(1,128)S(1)}, u32[]{:S(2)}, u32[]{:S(2)}) async-start(s32[16,1,1]{2,1,0:T(1,128)} %copy.29), calls=%async_computation.1 | async-start | bytes 16384 | tf_op jit(solution)/shard_map/all_to_all | solution.py:119
  20.5 3.9 %all-to-all-done.1 = s32[16,1,1]{2,1,0:T(1,128)S(1)} async-done(((s32[16,1,1]{2,1,0:T(1,128)}), s32[16,1,1]{2,1,0:T(1,128)S(1)}, u32[]{:S(2)}, u32[]{:S(2)}) %all-to-all-start.1) | async-done | bytes 96 | tf_op jit(solution)/shard_map/all_to_all | solution.py:119
  24.4 3.5 %all-to-all-start = ((bf16[16,2,165]{2,1,0:T(2,128)(2,1)}), bf16[16,2,165]{2,1,0:T(2,128)(2,1)S(1)}, u32[]{:S(2)}, u32[]{:S(2)}) async-start(bf16[16,2,165]{2,1,0:T(2,128)(2,1)} %reshape.261), calls=%async_computation | async-start | bytes 32768 | tf_op jit(solution)/shard_map/all_to_all | solution.py:118
  29.0 5.3 %all-to-all-done = bf16[16,2,165]{2,1,0:T(2,128)(2,1)S(1)} async-done(((bf16[16,2,165]{2,1,0:T(2,128)(2,1)}), bf16[16,2,165]{2,1,0:T(2,128)(2,1)S(1)}, u32[]{:S(2)}, u32[]{:S(2)}) %all-to-all-start) | async-done | bytes 10592 | tf_op jit(solution)/shard_map/all_to_all | solution.py:118
  35.0 41.1 %while.17 = (s32[]{:T(128)}, f32[16,512]{1,0:T(8,128)}, bf16[2,256,1536]{2,1,0:T(8,128)(2,1)}, bf16[2,256,512]{2,1,0:T(8,128)(2,1)}, bf16[2,8,330]{2,1,0:T(8,128...) while((s32[]{:T(128)}, f32[16,512]{1,0:T(8,128)}, ...), condition=%wide.region_15.16_spmd.clone, body=%wide.region_0.15_spmd.clone.sunk | while | flops 835685888 | bytes 56027588 | solution.py:148
  39.9 2.1 %fusion.59 = (f32[256]{0:T(256)S(1)}, f32[256,512]{1,0:T(8,128)S(1)}) fusion(f32[512]{0:T(512)S(1)} %copy-done.11, bf16[1536,512]{1,0:T(8,128)(2,1)} %get-tuple-element.475, bf16[256,512]{1,0:T(8,128)(2,1)S(1)} %bitcast.86, bf16[256,1024]{1,0:T(8,128)(2,1)S(1)} %concatenate.58), kind=kOutput, calls=%fused_computation.73.clone.1 | convolution fusion | flops 404487936 | bytes 2886656 | tf_op jit(solution)/shard_map/while/body/eval_jaxpr/dot_general | solution.py:64
  43.3 0.8 copy-done.10
  44.1 0.9 maximum_dynamic-update-slice_fusion.2
  45.1 0.8 copy-done.1
  46.4 0.8 slice_bitcast_fusion.2
  47.5 1.6 copy.42
  49.5 1.7 reshape.274
  51.2 1.5 pad_add_fusion.2
  52.9 1.1 multiply_reduce_fusion.15
  55.3 0.7 and_select_fusion.2
  60.1 2.1 %fusion.59 = (f32[256]{0:T(256)S(1)}, f32[256,512]{1,0:T(8,128)S(1)}) fusion(f32[512]{0:T(512)S(1)} %copy-done.11, bf16[1536,512]{1,0:T(8,128)(2,1)} %get-tuple-element.475, bf16[256,512]{1,0:T(8,128)(2,1)S(1)} %bitcast.86, bf16[256,1024]{1,0:T(8,128)(2,1)S(1)} %concatenate.58), kind=kOutput, calls=%fused_computation.73.clone.1 | convolution fusion | flops 404487936 | bytes 2886656 | tf_op jit(solution)/shard_map/while/body/eval_jaxpr/dot_general | solution.py:64
  63.5 0.8 copy-done.10
  64.3 0.9 maximum_dynamic-update-slice_fusion.2
  65.3 0.8 copy-done.1
  66.6 0.8 slice_bitcast_fusion.2
  67.7 1.6 copy.42
  69.7 1.7 reshape.274
  71.4 1.5 pad_add_fusion.2
  73.1 1.1 multiply_reduce_fusion.15
  74.8 1.4 select_add_fusion.2
  76.2 4.2 %convolution_bitcast_fusion = f32[1536,512]{1,0:T(8,128)} fusion(bf16[2,256,1536]{2,1,0:T(8,128)(2,1)} %get-tuple-element.190, bf16[2,256,512]{2,1,0:T(8,128)(2,1)} %get-tuple-element.191), kind=kOutput, calls=%fused_computation.65 | convolution fusion | flops 805306368 | bytes 5242880 | tf_op jit(solution)/shard_map/dot_general | solution.py:151
  81.0 63.6 %reduce-scatter.2.cloned.1.call-done = f32[96,512]{1,0:T(8,128)} async-done(((f32[1536,512]{1,0:T(8,128)}), f32[96,512]{1,0:T(8,128)}) %reduce-scatter.2.cloned.1.call-update) | async-done | bytes 196624 | tf_op jit(solution)/shard_map/reduce_scatter | solution.py:155
  144.7 1.6 all-gather.3.cloned.1.call-done
  146.3 1.9 %reduce_sum.177 = f32[16,512]{1,0:T(8,128)} reduce(f32[32,16,512]{2,1,0:T(8,128)} %bitcast.89, f32[]{:T(128)} %constant.127.clone.1), dimensions={0}, to_apply=%region_18.19 | reduce | flops 253952 | bytes 1081348 | tf_op jit(solution)/shard_map/reduce_sum | solution.py:156
  148.3 19.9 %all-reduce.5.cloned.1.call-done = f32[96,512]{1,0:T(8,128)} async-done(((f32[96,512]{1,0:T(8,128)}), f32[96,512]{1,0:T(8,128)}) %all-reduce.5.cloned.1.call-update) | async-done | bytes 196624 | tf_op jit(solution)/shard_map/psum | solution.py:154
  168.2 1.6 copy.58
  (138 shorter events, 22.1 us)
Async XLA Ops:
  8.0 10.1 %copy-start = (bf16[16,330]{1,0:T(8,128)(2,1)S(1)}, bf16[16,330]{1,0:T(8,128)(2,1)}, u32[]{:S(2)}) copy-start(bf16[16,330]{1,0:T(8,128)(2,1)} %param.14) | copy-start | bytes 31684
  10.7 13.7 %all-to-all-start.1 = ((s32[16,1,1]{2,1,0:T(1,128)}), s32[16,1,1]{2,1,0:T(1,128)S(1)}, u32[]{:S(2)}, u32[]{:S(2)}) async-start(s32[16,1,1]{2,1,0:T(1,128)} %copy.29), calls=%async_computation.1 | async-start | bytes 16384 | tf_op jit(solution)/shard_map/all_to_all | solution.py:119
  24.4 10.0 %all-to-all-start = ((bf16[16,2,165]{2,1,0:T(2,128)(2,1)}), bf16[16,2,165]{2,1,0:T(2,128)(2,1)S(1)}, u32[]{:S(2)}, u32[]{:S(2)}) async-start(bf16[16,2,165]{2,1,0:T(2,128)(2,1)} %reshape.261), calls=%async_computation | async-start | bytes 32768 | tf_op jit(solution)/shard_map/all_to_all | solution.py:118
  27.9 116.8 %reduce-scatter.2.cloned.1.call-start = ((), (), s32[]{:S(2)}) async-start(), calls=%async_computation.4 | async-start | bytes 3342336 | tf_op jit(solution)/shard_map/reduce_scatter | solution.py:155
  35.0 2.3 %copy-start.2 = (bf16[2,8,32,512]{3,2,1,0:T(8,128)(2,1)S(1)}, bf16[2,8,32,512]{3,2,1,0:T(8,128)(2,1)}, u32[]{:S(2)}) copy-start(bf16[2,8,32,512]{3,2,1,0:T(8,128)(2,1)} %get-tuple-element.477) | copy-start | bytes 1572868 | tf_op jit(solution)/shard_map/while
  35.1 2.3 %copy-start.4 = (bf16[10,512]{1,0:T(8,128)(2,1)S(1)}, bf16[10,512]{1,0:T(8,128)(2,1)}, u32[]{:S(2)}) copy-start(bf16[10,512]{1,0:T(8,128)(2,1)} %get-tuple-element.471) | copy-start | bytes 30724 | tf_op jit(solution)/shard_map/while
  35.1 2.3 %copy-start.7 = (f32[512]{0:T(512)S(1)}, f32[512]{0:T(512)}, u32[]{:S(2)}) copy-start(f32[512]{0:T(512)} %get-tuple-element.472) | copy-start | bytes 6148 | tf_op jit(solution)/shard_map/while
  37.4 0.8 copy-start.3
  37.4 0.8 copy-start.5
  39.2 0.7 copy-start.11
  39.9 2.3 %copy-start.6 = (f32[512]{0:T(512)S(1)}, f32[512]{0:T(512)}, u32[]{:S(2)}) copy-start(f32[512]{0:T(512)} %get-tuple-element.479) | copy-start | bytes 6148 | tf_op jit(solution)/shard_map/while
  39.9 2.3 %copy-start.8 = (f32[512]{0:T(512)S(1)}, f32[512]{0:T(512)}, u32[]{:S(2)}) copy-start(f32[512]{0:T(512)} %get-tuple-element.480) | copy-start | bytes 6148 | tf_op jit(solution)/shard_map/while
  42.0 1.0 copy-start.9
  43.3 0.8 copy-start.10
  44.1 1.7 copy-start.1
  55.2 2.3 %copy-start.2 = (bf16[2,8,32,512]{3,2,1,0:T(8,128)(2,1)S(1)}, bf16[2,8,32,512]{3,2,1,0:T(8,128)(2,1)}, u32[]{:S(2)}) copy-start(bf16[2,8,32,512]{3,2,1,0:T(8,128)(2,1)} %get-tuple-element.477) | copy-start | bytes 1572868 | tf_op jit(solution)/shard_map/while
  55.2 2.3 %copy-start.4 = (bf16[10,512]{1,0:T(8,128)(2,1)S(1)}, bf16[10,512]{1,0:T(8,128)(2,1)}, u32[]{:S(2)}) copy-start(bf16[10,512]{1,0:T(8,128)(2,1)} %get-tuple-element.471) | copy-start | bytes 30724 | tf_op jit(solution)/shard_map/while
  55.3 2.3 %copy-start.7 = (f32[512]{0:T(512)S(1)}, f32[512]{0:T(512)}, u32[]{:S(2)}) copy-start(f32[512]{0:T(512)} %get-tuple-element.472) | copy-start | bytes 6148 | tf_op jit(solution)/shard_map/while
  57.6 0.8 copy-start.3
  57.6 0.8 copy-start.5
  59.4 0.7 copy-start.11
  60.1 2.3 %copy-start.6 = (f32[512]{0:T(512)S(1)}, f32[512]{0:T(512)}, u32[]{:S(2)}) copy-start(f32[512]{0:T(512)} %get-tuple-element.479) | copy-start | bytes 6148 | tf_op jit(solution)/shard_map/while
  60.1 2.3 %copy-start.8 = (f32[512]{0:T(512)S(1)}, f32[512]{0:T(512)}, u32[]{:S(2)}) copy-start(f32[512]{0:T(512)} %get-tuple-element.480) | copy-start | bytes 6148 | tf_op jit(solution)/shard_map/while
  62.2 1.0 copy-start.9
  63.4 0.8 copy-start.10
  64.3 1.7 copy-start.1
  80.4 65.9 %all-gather.3.cloned.1.call-start = ((), (), s32[]{:S(2)}) async-start(), calls=%async_computation.3 | async-start | bytes 1081344 | tf_op jit(solution)/shard_map/all_gather | solution.py:156
  81.0 87.2 %all-reduce.5.cloned.1.call-start = ((), (), s32[]{:S(2)}) async-start(), calls=%async_computation.5 | async-start | bytes 393216 | tf_op jit(solution)/shard_map/psum | solution.py:154
Sparse Core Ops, SparseCore 0:
  80.5 64.1 reduce-scatter.1
  147.0 21.1 all-reduce.4
Sparse Core Ops, SparseCore 1:
  84.4 61.8 all-gather.2
